TPU v7x, 32 devices: a whole 2x2x4 slice. The times are simulated.
32 devices in a mesh: rcv: 4 (over y, core), src: 8 (over z, x).
Axes of the slice: x: 2, y: 2, z: 4, core: 2. Of those that a mesh axis runs over, the one named last changes fastest.
Arguments:
- pplus: bfloat16 [2048, 2, 1024], P('rcv', None, 'src'), may hold values from -0.125 to 0.125
- pminus: bfloat16 [2048, 2, 1024], P('rcv', None, 'src')
- band: int32 [8, 3], P('rcv'), may hold values from 0 to 7, as said below
Outputs:
- reflectivity: float32 [256, 8, 3, 2, 256], P('src', 'rcv')
- misfit: float32 [2048, 2, 1024], P('rcv', None, 'src')
Inputs may be any that keep to these rules, and one draw needn't show every extreme that they name: `band`: row b names block b first and then 3 - 1 other distinct blocks, each at most 2 blocks from b.
All inputs are finite; a program needn't handle non-finite values.
Results may differ from a plain program's by a relative error of at most 0.024.
Values may be sent and summed in bfloat16 or wider, within the bound.
No kernel may reach another device: no remote copies, remote signals or barrier semaphores. Data moves between devices by JAX's collectives and lax.ppermute only.
A program may use at most 64 MiB of HBM per device.

v0:
```python
import functools

import jax
import jax.numpy as jnp
from jax import lax
from jax.experimental import pallas as pl
from jax.experimental.pallas import tpu as pltpu
from jax.sharding import PartitionSpec as P

BLOCK = 256
NEIGH = 3
HALO_BLK = 2
ROWS_X = 2
SHARE_ROWS = 16


def ring_order(count):
    if count % ROWS_X or count < 2 * ROWS_X:
        return list(range(count))
    half = count // ROWS_X
    return [ROWS_X * p for p in range(half)] + [ROWS_X * p + 1 for p in reversed(range(half))]


def ring_place(count, index, shift):
    if count % ROWS_X or count < 2 * ROWS_X:
        return lax.rem(index + shift + count, count)
    half, odd = count // ROWS_X, lax.rem(index, ROWS_X)
    step = (index - odd) // ROWS_X
    place = lax.rem(jnp.where(odd == 1, count - 1 - step, step) + shift + count, count)
    return jnp.where(place < half, ROWS_X * place, ROWS_X * (count - 1 - place) + 1)


def along(sums):
    total = jnp.sum(sums, axis=1, keepdims=True)
    qq, qw = total[1:2], total[4:5]
    return jnp.where(qq > 0, qw / jnp.where(qq > 0, qq, 1.0), 0.0)


def maps_kernel(n_src, shifts, *refs):
    me, band, field = refs[:3]
    ends = [3, 3 + n_src, 3 + 2 * n_src, 3 + 3 * n_src]
    sources = [refs[a:b] for a, b in zip(ends[:-1], ends[1:])]
    grad, hess, images, sums_out = refs[ends[3] : ends[3] + 4]
    held, lhs, every, factors, image0, image1, sems = refs[ends[3] + 4 :]
    blocks_here = grad.shape[0]
    rows = grad.shape[1] // 2
    cols = field.shape[2]
    half = cols // 2
    window = blocks_here * len(sources)
    me_rcv, me_src = me[0], me[1]
    odd = lax.rem(me_rcv, 2)
    where = [ring_place(n_src, me_src, shift) for shift in shifts]

    fetches = [
        [pltpu.make_async_copy(chunk, held.at[g, slot], sems.at[g, slot]) for slot, chunk in enumerate(group)]
        for g, group in enumerate(sources)
    ]
    for fetch in sum(fetches, []):
        fetch.start()

    places = {}
    for i in range(blocks_here):
        for k in range(NEIGH):
            offset = band[i, k] - me_rcv * blocks_here
            before, here = offset < 0, (offset >= 0) & (offset < blocks_here)
            group = jnp.where(here, 0, jnp.where(jnp.where(before, 1, 0) == odd, 1, 2))
            inside = jnp.where(before, offset + blocks_here, jnp.where(here, offset, offset - blocks_here))
            places[i, k] = group * blocks_here + inside

    def block(place, slot):
        start = place % blocks_here * BLOCK
        return held[place // blocks_here, slot, start : start + BLOCK, :]

    def store(i, slot, re_bf, im_bf):
        top, low = slice(2 * i * rows, (2 * i + 1) * rows), slice((2 * i + 1) * rows, (2 * i + 2) * rows)
        left, right = slice(slot * cols, slot * cols + half), slice(slot * cols + half, (slot + 1) * cols)
        lhs[top, left] = re_bf
        lhs[top, right] = im_bf
        lhs[low, left] = im_bf
        lhs[low, right] = -re_bf

    def fold(x):
        total = x[:, :128]
        for c in range(128, x.shape[1], 128):
            total = total + x[:, c : c + 128]
        return jnp.sum(total, axis=0, keepdims=True)

    def adjoint(out, first):
        for place in range(window):
            if first and place % blocks_here == 0:
                for fetch in fetches[place // blocks_here]:
                    fetch.wait()
            row = jnp.concatenate([block(place, slot) for slot in range(n_src)], axis=1)
            every[place] = lax.dot_general(
                lhs[...], row, (((1,), (1,)), ((), ())), preferred_element_type=jnp.float32
            )
        for i in range(blocks_here):
            mine = slice(2 * i * rows, 2 * (i + 1) * rows)
            for k in range(NEIGH):
                part = every[places[i, k], mine, :]
                out[i, :, k * BLOCK : (k + 1) * BLOCK] = part
                factors[places[i, k], mine, :] = part.astype(jnp.bfloat16)

    def forward(slot):
        column = jnp.concatenate([block(place, slot) for place in range(window)], axis=0)
        wide = jnp.concatenate([factors[place] for place in range(window)], axis=1)
        prod = jnp.dot(wide, column, preferred_element_type=jnp.float32)
        for i in range(blocks_here):
            top, low = prod[2 * i * rows : (2 * i + 1) * rows], prod[(2 * i + 1) * rows : 2 * (i + 1) * rows]
            yield i, top[:, :half] - low[:, half:], top[:, half:] + low[:, :half]

    factors[...] = jnp.zeros_like(factors)
    for slot in range(n_src):
        for i in range(blocks_here):
            rows_bf = field[where[slot], i * rows : (i + 1) * rows, :]
            store(i, slot, rows_bf[:, :half], rows_bf[:, half:])

    zero = jnp.zeros((1, 128), jnp.float32)
    gg, qq, gh, hh, qw, ww = zero, zero, zero, zero, zero, zero
    adjoint(grad, True)
    for i in range(blocks_here):
        gg += fold(grad[i] * grad[i])
    for slot in range(n_src):
        for i, re, im in forward(slot):
            mine = slice(i * rows, (i + 1) * rows)
            qq += fold(re * re + im * im)
            image0[slot, mine, :half] = re
            image0[slot, mine, half:] = im
            store(i, slot, re.astype(jnp.bfloat16), im.astype(jnp.bfloat16))
    adjoint(hess, False)
    for i in range(blocks_here):
        gh += fold(hess[i] * grad[i])
        hh += fold(hess[i] * hess[i])
    for slot in range(n_src):
        for i, re, im in forward(slot):
            mine = slice(i * rows, (i + 1) * rows)
            ww += fold(re * re + im * im)
            qw += fold(re * image0[slot, mine, :half] + im * image0[slot, mine, half:])
            image1[slot, mine, :half] = re
            image1[slot, mine, half:] = im
    sums = jnp.concatenate([gg, qq, gh, hh, qw, ww, zero, zero], axis=0)
    sums_out[...] = sums
    share_bf = along(sums).astype(jnp.bfloat16)
    share = share_bf.astype(jnp.float32)
    height = blocks_here * rows
    for slot in range(n_src):
        first = image0[slot]
        images[where[slot], :height] = first.astype(jnp.bfloat16)
        images[where[slot], height : 2 * height] = (image1[slot] - share * first).astype(jnp.bfloat16)
        images[where[slot], 2 * height :] = jnp.broadcast_to(share_bf, (SHARE_ROWS, cols))


def combine_kernel(sums, images, grad, hess, refl_out, moved_out):
    n_src, height = images.shape[0], (images.shape[1] - SHARE_ROWS) // 2
    total = jnp.sum(sums[...], axis=1, keepdims=True)
    gg, qq, gh, hh, qw, ww = [total[i : i + 1] for i in range(6)]
    step0 = gg / qq
    grad_next = gg - 2 * step0 * gh + step0 * step0 * hh
    near = 1 + grad_next / gg
    image_sq = near * near * qq - 2 * near * step0 * qw + step0 * step0 * ww
    step1 = grad_next / image_sq
    c1 = step0 + step1 * near
    c2 = -step0 * step1
    for i in range(grad.shape[0]):
        refl_out[i] = c1 * grad[i] + c2 * hess[i]
    for s in range(n_src):
        share = images[s, 2 * height :].astype(jnp.float32)[:1, :1]
        first = images[s, :height].astype(jnp.float32)
        rest = images[s, height : 2 * height].astype(jnp.float32)
        moved_out[s] = (c1 + c2 * share) * first + c2 * rest


def summed(x, axis, count):
    if count & (count - 1):
        return lax.psum(x, axis)
    bit = 1
    while bit < count:
        radix = min(4, count // bit)
        others = [lax.ppermute(x, axis, [(d, d ^ (bit * m)) for d in range(count)]) for m in range(1, radix)]
        x = (x + others[0]) + (others[1] + others[2]) if radix == 4 else x + others[0]
        bit *= radix
    return x


def per_device(n_rcv, n_src, pplus, pminus, band):
    blocks_here = band.shape[0]
    rows = BLOCK // n_src
    cols = 2 * pplus.shape[2]
    order = ring_order(n_src)
    ahead = [(order[p], order[(p + 1) % n_src]) for p in range(n_src)]
    behind = [(d, s) for s, d in ahead]

    def swaps(first):
        pairs = [(r, r + 1) for r in range(first, n_rcv - 1, 2)]
        return pairs + [(d, s) for s, d in pairs]

    start = lax.optimization_barrier(pminus.reshape(blocks_here * BLOCK, cols))
    start = jnp.transpose(start.reshape(blocks_here, n_src, rows, cols), (1, 0, 2, 3))
    field = lax.all_to_all(start.reshape(n_src, blocks_here * rows, cols), "src", 0, 0, tiled=True)

    own = pplus.reshape(blocks_here * BLOCK, cols)
    chunks, shifts = [own], [0]
    fwd = bwd = own
    for step in range(1, n_src // 2 + 1):
        fwd = lax.ppermute(fwd, "src", ahead)
        chunks.append(fwd)
        shifts.append(-step)
        if len(chunks) < n_src:
            bwd = lax.ppermute(bwd, "src", behind)
            chunks.append(bwd)
            shifts.append(step)
    near = [lax.ppermute(c, "rcv", swaps(0)) for c in chunks]
    far = [lax.ppermute(c, "rcv", swaps(1)) for c in chunks]
    me = jnp.stack([lax.axis_index("rcv"), lax.axis_index("src")]).astype(jnp.int32)

    any_spec = pl.BlockSpec(memory_space=pl.ANY)
    smem, vmem = pl.BlockSpec(memory_space=pltpu.SMEM), pl.BlockSpec(memory_space=pltpu.VMEM)
    band_cols = NEIGH * BLOCK
    grad, hess, images, sums = pl.pallas_call(
        functools.partial(maps_kernel, n_src, shifts),
        out_shape=(
            jax.ShapeDtypeStruct((blocks_here, 2 * rows, band_cols), jnp.float32),
            jax.ShapeDtypeStruct((blocks_here, 2 * rows, band_cols), jnp.float32),
            jax.ShapeDtypeStruct((n_src, 2 * blocks_here * rows + SHARE_ROWS, cols), jnp.bfloat16),
            jax.ShapeDtypeStruct((8, 128), jnp.float32),
        ),
        in_specs=[smem, smem, vmem] + [any_spec] * (3 * n_src),
        out_specs=[vmem] * 4,
        scratch_shapes=[
            pltpu.VMEM((3, n_src, blocks_here * BLOCK, cols), jnp.bfloat16),
            pltpu.VMEM((blocks_here * 2 * rows, n_src * cols), jnp.bfloat16),
            pltpu.VMEM((3 * blocks_here, blocks_here * 2 * rows, BLOCK), jnp.float32),
            pltpu.VMEM((3 * blocks_here, blocks_here * 2 * rows, BLOCK), jnp.bfloat16),
            pltpu.VMEM((n_src, blocks_here * rows, cols), jnp.float32),
            pltpu.VMEM((n_src, blocks_here * rows, cols), jnp.float32),
            pltpu.SemaphoreType.DMA((3, n_src)),
        ],
        compiler_params=pltpu.CompilerParams(vmem_limit_bytes=60 << 20),
        name="maps",
    )(me, band, field, *chunks, *near, *far)

    images = lax.all_to_all(images, "src", 0, 0, tiled=True)
    sums = summed(summed(sums, "rcv", n_rcv), "src", n_src)
    refl, moved = pl.pallas_call(
        combine_kernel,
        out_shape=(
            jax.ShapeDtypeStruct(grad.shape, jnp.float32),
            jax.ShapeDtypeStruct((n_src, blocks_here * rows, cols), jnp.float32),
        ),
        in_specs=[vmem] * 4,
        out_specs=[vmem] * 2,
        compiler_params=pltpu.CompilerParams(vmem_limit_bytes=8 << 20),
        name="combine",
    )(sums, images, grad, hess)

    refl = jnp.transpose(refl.reshape(blocks_here, 2, rows, NEIGH, BLOCK), (2, 0, 3, 1, 4))
    moved = jnp.transpose(moved.reshape(n_src, blocks_here, rows, cols), (1, 0, 2, 3))
    misfit = pminus.astype(jnp.float32) - moved.reshape(pminus.shape)
    return refl, misfit


def solution(mesh):
    return jax.shard_map(
        functools.partial(per_device, mesh.shape["rcv"], mesh.shape["src"]),
        mesh=mesh,
        in_specs=(P("rcv", None, "src"), P("rcv", None, "src"), P("rcv", None)),
        out_specs=(P("src", "rcv", None, None, None), P("rcv", None, "src")),
        check_vma=False,
    )
```

profile of v0, /device:TPU:0, one launch (start us, length us, event | category | flops | bytes accessed | tf_op | source)
XLA Modules:
  0.0 85.8 jit_solution(4392519218467862500)
XLA Ops:
  1.7 3.0 %collective-permute-start.1 = (bf16[512,256]{1,0:T(8,128)(2,1)S(1)}, bf16[512,256]{1,0:T(8,128)(2,1)S(1)}, u32[]{:S(2)}, u32[]{:S(2)}) collective-permute-start(bf16[512,256]{1,0:T(8,128)(2,1)S(1)} %bitcast.28), channel_id=1, source_target_pairs={{2,0},{4,2},{6,4},{7,6},{5,7},{3,5},{1,3},{0,1},{10,8},{12,10},{14... | collective-permute-start | bytes 786440 | tf_op jit(solution)/shard_map/ppermute | solution.py:209
  5.5 3.3 %collective-permute-start.7 = (bf16[512,256]{1,0:T(8,128)(2,1)S(1)}, bf16[512,256]{1,0:T(8,128)(2,1)S(1)}, u32[]{:S(2)}, u32[]{:S(2)}) collective-permute-start(bf16[512,256]{1,0:T(8,128)(2,1)S(1)} %bitcast.31), channel_id=1, source_target_pairs={{0,8},{16,24},{8,0},{24,16},{1,9},{17,25},{9,1},{25,17},{2,10},{18... | collective-permute-start | bytes 786440 | tf_op jit(solution)/shard_map/ppermute | solution.py:212
  8.8 2.3 %collective-permute-done.1.refs_5_ = bf16[512,256]{1,0:T(8,128)(2,1)S(1)} collective-permute-done((bf16[512,256]{1,0:T(8,128)(2,1)S(1)}, bf16[512,256]{1,0:T(8,128)(2,1)S(1)}, u32[]{:S(2)}, u32[]{:S(2)}) %collective-permute-start.1) | collective-permute-done | bytes 262176 | tf_op jit(solution)/shard_map/ppermute | solution.py:209
  11.7 1.7 %collective-permute-start.3 = (bf16[512,256]{1,0:T(8,128)(2,1)S(1)}, bf16[512,256]{1,0:T(8,128)(2,1)S(1)}, u32[]{:S(2)}, u32[]{:S(2)}) collective-permute-start(bf16[512,256]{1,0:T(8,128)(2,1)S(1)} %collective-permute-done.1.refs_5_), channel_id=1, source_target_pairs={{2,0},{4,2},{6,4},{7,6},{5,7},{3,5},{1,3},{0,1},{10,8},{12,10},{14... | collective-permute-start | bytes 786440 | tf_op jit(solution)/shard_map/ppermute | solution.py:209
  13.8 2.5 %collective-permute-start.9 = (bf16[512,256]{1,0:T(8,128)(2,1)S(1)}, bf16[512,256]{1,0:T(8,128)(2,1)S(1)}, u32[]{:S(2)}, u32[]{:S(2)}) collective-permute-start(bf16[512,256]{1,0:T(8,128)(2,1)S(1)} %collective-permute-done.1.refs_5_), channel_id=1, source_target_pairs={{0,8},{16,24},{8,0},{24,16},{1,9},{17,25},{9,1},{25,17},{2,10},{18... | collective-permute-start | bytes 786440 | tf_op jit(solution)/shard_map/ppermute | solution.py:212
  17.0 2.1 %collective-permute-start.8 = (bf16[512,256]{1,0:T(8,128)(2,1)S(1)}, bf16[512,256]{1,0:T(8,128)(2,1)S(1)}, u32[]{:S(2)}, u32[]{:S(2)}) collective-permute-start(bf16[512,256]{1,0:T(8,128)(2,1)S(1)} %collective-permute-done.refs_4_), channel_id=1, source_target_pairs={{0,8},{16,24},{8,0},{24,16},{1,9},{17,25},{9,1},{25,17},{2,10},{18... | collective-permute-start | bytes 786440 | tf_op jit(solution)/shard_map/ppermute | solution.py:212
  21.5 1.5 %collective-permute-start.5 = (bf16[512,256]{1,0:T(8,128)(2,1)S(1)}, bf16[512,256]{1,0:T(8,128)(2,1)}, u32[]{:S(2)}, u32[]{:S(2)}) collective-permute-start(bf16[512,256]{1,0:T(8,128)(2,1)S(1)} %collective-permute-done.3.refs_7_), channel_id=1, source_target_pairs={{2,0},{4,2},{6,4},{7,6},{5,7},{3,5},{1,3},{0,1},{10,8},{12,10},{14... | collective-permute-start | bytes 786440 | tf_op jit(solution)/shard_map/ppermute | solution.py:209
  23.0 1.7 %collective-permute-start.11 = (bf16[512,256]{1,0:T(8,128)(2,1)S(1)}, bf16[512,256]{1,0:T(8,128)(2,1)}, u32[]{:S(2)}, u32[]{:S(2)}) collective-permute-start(bf16[512,256]{1,0:T(8,128)(2,1)S(1)} %collective-permute-done.3.refs_7_), channel_id=1, source_target_pairs={{0,8},{16,24},{8,0},{24,16},{1,9},{17,25},{9,1},{25,17},{2,10},{18... | collective-permute-start | bytes 786440 | tf_op jit(solution)/shard_map/ppermute | solution.py:212
  24.7 1.4 %collective-permute-start.18 = (bf16[512,256]{1,0:T(8,128)(2,1)S(1)}, bf16[512,256]{1,0:T(8,128)(2,1)}, u32[]{:S(2)}, u32[]{:S(2)}) collective-permute-start(bf16[512,256]{1,0:T(8,128)(2,1)S(1)} %collective-permute-done.2.refs_6_), channel_id=1, source_target_pairs={{8,16},{16,8},{9,17},{17,9},{10,18},{18,10},{11,19},{19,11},{12,20... | collective-permute-start | bytes 786440 | tf_op jit(solution)/shard_map/ppermute | solution.py:213
  26.0 3.0 %collective-permute-start.10 = (bf16[512,256]{1,0:T(8,128)(2,1)S(1)}, bf16[512,256]{1,0:T(8,128)(2,1)}, u32[]{:S(2)}, u32[]{:S(2)}) collective-permute-start(bf16[512,256]{1,0:T(8,128)(2,1)S(1)} %collective-permute-done.2.refs_6_), channel_id=1, source_target_pairs={{0,8},{16,24},{8,0},{24,16},{1,9},{17,25},{9,1},{25,17},{2,10},{18... | collective-permute-start | bytes 786440 | tf_op jit(solution)/shard_map/ppermute | solution.py:212
  29.1 1.3 %collective-permute-start.6 = (bf16[512,256]{1,0:T(8,128)(2,1)}, bf16[512,256]{1,0:T(8,128)(2,1)}, u32[]{:S(2)}, u32[]{:S(2)}) collective-permute-start(bf16[512,256]{1,0:T(8,128)(2,1)} %collective-permute-done.4.refs_8_), channel_id=1, source_target_pairs={{0,2},{2,4},{4,6},{6,7},{7,5},{5,3},{3,1},{1,0},{8,10},{10,12},{12... | collective-permute-start | bytes 786440 | tf_op jit(solution)/shard_map/ppermute | solution.py:205
  30.4 1.4 %collective-permute-start.21 = (bf16[512,256]{1,0:T(8,128)(2,1)}, bf16[512,256]{1,0:T(8,128)(2,1)}, u32[]{:S(2)}, u32[]{:S(2)}) collective-permute-start(bf16[512,256]{1,0:T(8,128)(2,1)} %collective-permute-done.5.refs_9_), channel_id=1, source_target_pairs={{8,16},{16,8},{9,17},{17,9},{10,18},{18,10},{11,19},{19,11},{12,20... | collective-permute-start | bytes 786440 | tf_op jit(solution)/shard_map/ppermute | solution.py:213
  32.6 5.3 %all-to-all-start = ((bf16[8,64,256]{2,1,0:T(8,128)(2,1)}), bf16[8,64,256]{2,1,0:T(8,128)(2,1)S(1)}, u32[]{:S(2)}, u32[]{:S(2)}) async-start(bf16[8,64,256]{2,1,0:T(8,128)(2,1)} %bitcast.4), calls=%async_computation | async-start | bytes 524288 | tf_op jit(solution)/shard_map/all_to_all | solution.py:199
  37.9 2.3 %collective-permute-start.13 = (bf16[512,256]{1,0:T(8,128)(2,1)}, bf16[512,256]{1,0:T(8,128)(2,1)S(1)}, u32[]{:S(2)}, u32[]{:S(2)}) collective-permute-start(bf16[512,256]{1,0:T(8,128)(2,1)} %collective-permute-done.5.refs_9_), channel_id=1, source_target_pairs={{0,8},{16,24},{8,0},{24,16},{1,9},{17,25},{9,1},{25,17},{2,10},{18... | collective-permute-start | bytes 786440 | tf_op jit(solution)/shard_map/ppermute | solution.py:212
  40.9 2.1 %collective-permute-start.12 = (bf16[512,256]{1,0:T(8,128)(2,1)}, bf16[512,256]{1,0:T(8,128)(2,1)S(1)}, u32[]{:S(2)}, u32[]{:S(2)}) collective-permute-start(bf16[512,256]{1,0:T(8,128)(2,1)} %collective-permute-done.4.refs_8_), channel_id=1, source_target_pairs={{0,8},{16,24},{8,0},{24,16},{1,9},{17,25},{9,1},{25,17},{2,10},{18... | collective-permute-start | bytes 786440 | tf_op jit(solution)/shard_map/ppermute | solution.py:212
  43.7 2.3 %collective-permute-start.14 = (bf16[512,256]{1,0:T(8,128)(2,1)}, bf16[512,256]{1,0:T(8,128)(2,1)S(1)}, u32[]{:S(2)}, u32[]{:S(2)}) collective-permute-start(bf16[512,256]{1,0:T(8,128)(2,1)} %collective-permute-done.6.refs_10_), channel_id=1, source_target_pairs={{0,8},{16,24},{8,0},{24,16},{1,9},{17,25},{9,1},{25,17},{2,10},{18... | collective-permute-start | bytes 786440 | tf_op jit(solution)/shard_map/ppermute | solution.py:212
  48.4 10.2 %maps.1 = (f32[2,64,768]{2,1,0:T(8,128)}, f32[2,64,768]{2,1,0:T(8,128)}, bf16[8,144,256]{2,1,0:T(8,128)(2,1)}, f32[8,128]{1,0:T(8,128)}) custom-call(s32[2]{0:T(128)} %pad_add_fusion.refs_0_, s32[2,3]{1,0:T(2,128)} %refs_1_.1, bf16[8,64,256]{2,1,0:T(8,128)(2,1)} %copy-done.4, bf16[512,256]{1,0:T(8,128)(2,1)} %bitcast.32, bf16[512,256]{1,0:T(8,128)(2,1)} %copy-done.6, ...), custom_call_target="tpu_custom_call" | custom-call | tf_op jit(solution)/shard_map/maps/pallas_call | solution.py:219
  58.7 5.7 %all-to-all-start.1 = ((bf16[8,144,256]{2,1,0:T(8,128)(2,1)}), bf16[8,144,256]{2,1,0:T(8,128)(2,1)S(1)}, u32[]{:S(2)}, u32[]{:S(2)}) async-start(bf16[8,144,256]{2,1,0:T(8,128)(2,1)} %get-tuple-element.9), calls=%async_computation.1 | async-start | bytes 1179648 | tf_op jit(solution)/shard_map/all_to_all | solution.py:242
  65.3 4.8 %collective-permute-start.24 = (f32[8,128]{1,0:T(8,128)S(1)}, f32[8,128]{1,0:T(8,128)S(1)}, u32[]{:S(2)}, u32[]{:S(2)}) collective-permute-start(f32[8,128]{1,0:T(8,128)S(1)} %copy-done.21), channel_id=1, source_target_pairs={{0,16},{8,24},{16,0},{24,8},{1,17},{9,25},{17,1},{25,9},{2,18},{10... | collective-permute-start | bytes 12296 | tf_op jit(solution)/shard_map/ppermute | solution.py:179
  70.1 1.6 %collective-permute-done.24 = f32[8,128]{1,0:T(8,128)S(1)} collective-permute-done((f32[8,128]{1,0:T(8,128)S(1)}, f32[8,128]{1,0:T(8,128)S(1)}, u32[]{:S(2)}, u32[]{:S(2)}) %collective-permute-start.24) | collective-permute-done | bytes 4128 | tf_op jit(solution)/shard_map/ppermute | solution.py:179
  71.7 2.6 %collective-permute-start.28 = (f32[8,128]{1,0:T(8,128)S(1)}, f32[8,128]{1,0:T(8,128)S(1)}, u32[]{:S(2)}, u32[]{:S(2)}) collective-permute-start(f32[8,128]{1,0:T(8,128)S(1)} %add_add_fusion.1), channel_id=1, source_target_pairs={{0,3},{1,2},{2,1},{3,0},{4,7},{5,6},{6,5},{7,4},{8,11},{9,10},{10,... | collective-permute-start | bytes 12296 | tf_op jit(solution)/shard_map/ppermute | solution.py:179
  76.3 1.7 %collective-permute-done.27 = f32[8,128]{1,0:T(8,128)S(1)} collective-permute-done((f32[8,128]{1,0:T(8,128)S(1)}, f32[8,128]{1,0:T(8,128)S(1)}, u32[]{:S(2)}, u32[]{:S(2)}) %collective-permute-start.27) | collective-permute-done | bytes 4128 | tf_op jit(solution)/shard_map/ppermute | solution.py:179
  78.5 2.4 %collective-permute-start.29 = (f32[8,128]{1,0:T(8,128)S(1)}, f32[8,128]{1,0:T(8,128)S(1)}, u32[]{:S(2)}, u32[]{:S(2)}) collective-permute-start(f32[8,128]{1,0:T(8,128)S(1)} %add_add_fusion), channel_id=1, source_target_pairs={{0,4},{1,5},{2,6},{3,7},{4,0},{5,1},{6,2},{7,3},{8,12},{9,13},{10,... | collective-permute-start | bytes 12296 | tf_op jit(solution)/shard_map/ppermute | solution.py:179
  80.9 2.1 %collective-permute-done.29 = f32[8,128]{1,0:T(8,128)S(1)} collective-permute-done((f32[8,128]{1,0:T(8,128)S(1)}, f32[8,128]{1,0:T(8,128)S(1)}, u32[]{:S(2)}, u32[]{:S(2)}) %collective-permute-start.29) | collective-permute-done | bytes 4128 | tf_op jit(solution)/shard_map/ppermute | solution.py:179
  (98 shorter events, 16.6 us)
Async XLA Ops:
  1.7 9.4 %collective-permute-start.1 = (bf16[512,256]{1,0:T(8,128)(2,1)S(1)}, bf16[512,256]{1,0:T(8,128)(2,1)S(1)}, u32[]{:S(2)}, u32[]{:S(2)}) collective-permute-start(bf16[512,256]{1,0:T(8,128)(2,1)S(1)} %bitcast.28), channel_id=1, source_target_pairs={{2,0},{4,2},{6,4},{7,6},{5,7},{3,5},{1,3},{0,1},{10,8},{12,10},{14... | collective-permute-start | bytes 786440 | tf_op jit(solution)/shard_map/ppermute | solution.py:209
  4.7 8.8 %collective-permute-start = (bf16[512,256]{1,0:T(8,128)(2,1)S(1)}, bf16[512,256]{1,0:T(8,128)(2,1)S(1)}, u32[]{:S(2)}, u32[]{:S(2)}) collective-permute-start(bf16[512,256]{1,0:T(8,128)(2,1)S(1)} %bitcast.29), channel_id=1, source_target_pairs={{0,2},{2,4},{4,6},{6,7},{7,5},{5,3},{3,1},{1,0},{8,10},{10,12},{12... | collective-permute-start | bytes 786440 | tf_op jit(solution)/shard_map/ppermute | solution.py:205
  4.8 9.0 %collective-permute-start.15 = (bf16[512,256]{1,0:T(8,128)(2,1)S(1)}, bf16[512,256]{1,0:T(8,128)(2,1)S(1)}, u32[]{:S(2)}, u32[]{:S(2)}) collective-permute-start(bf16[512,256]{1,0:T(8,128)(2,1)S(1)} %bitcast.30), channel_id=1, source_target_pairs={{8,16},{16,8},{9,17},{17,9},{10,18},{18,10},{11,19},{19,11},{12,20... | collective-permute-start | bytes 786440 | tf_op jit(solution)/shard_map/ppermute | solution.py:213
  5.5 10.8 %collective-permute-start.7 = (bf16[512,256]{1,0:T(8,128)(2,1)S(1)}, bf16[512,256]{1,0:T(8,128)(2,1)S(1)}, u32[]{:S(2)}, u32[]{:S(2)}) collective-permute-start(bf16[512,256]{1,0:T(8,128)(2,1)S(1)} %bitcast.31), channel_id=1, source_target_pairs={{0,8},{16,24},{8,0},{24,16},{1,9},{17,25},{9,1},{25,17},{2,10},{18... | collective-permute-start | bytes 786440 | tf_op jit(solution)/shard_map/ppermute | solution.py:212
  11.1 5.9 %collective-permute-start.17 = (bf16[512,256]{1,0:T(8,128)(2,1)S(1)}, bf16[512,256]{1,0:T(8,128)(2,1)S(1)}, u32[]{:S(2)}, u32[]{:S(2)}) collective-permute-start(bf16[512,256]{1,0:T(8,128)(2,1)S(1)} %collective-permute-done.1.refs_5_), channel_id=1, source_target_pairs={{8,16},{16,8},{9,17},{17,9},{10,18},{18,10},{11,19},{19,11},{12,20... | collective-permute-start | bytes 786440 | tf_op jit(solution)/shard_map/ppermute | solution.py:213
  11.7 7.4 %collective-permute-start.3 = (bf16[512,256]{1,0:T(8,128)(2,1)S(1)}, bf16[512,256]{1,0:T(8,128)(2,1)S(1)}, u32[]{:S(2)}, u32[]{:S(2)}) collective-permute-start(bf16[512,256]{1,0:T(8,128)(2,1)S(1)} %collective-permute-done.1.refs_5_), channel_id=1, source_target_pairs={{2,0},{4,2},{6,4},{7,6},{5,7},{3,5},{1,3},{0,1},{10,8},{12,10},{14... | collective-permute-start | bytes 786440 | tf_op jit(solution)/shard_map/ppermute | solution.py:209
  13.5 7.5 %collective-permute-start.2 = (bf16[512,256]{1,0:T(8,128)(2,1)S(1)}, bf16[512,256]{1,0:T(8,128)(2,1)S(1)}, u32[]{:S(2)}, u32[]{:S(2)}) collective-permute-start(bf16[512,256]{1,0:T(8,128)(2,1)S(1)} %collective-permute-done.refs_4_), channel_id=1, source_target_pairs={{0,2},{2,4},{4,6},{6,7},{7,5},{5,3},{3,1},{1,0},{8,10},{10,12},{12... | collective-permute-start | bytes 786440 | tf_op jit(solution)/shard_map/ppermute | solution.py:205
  13.8 7.7 %collective-permute-start.9 = (bf16[512,256]{1,0:T(8,128)(2,1)S(1)}, bf16[512,256]{1,0:T(8,128)(2,1)S(1)}, u32[]{:S(2)}, u32[]{:S(2)}) collective-permute-start(bf16[512,256]{1,0:T(8,128)(2,1)S(1)} %collective-permute-done.1.refs_5_), channel_id=1, source_target_pairs={{0,8},{16,24},{8,0},{24,16},{1,9},{17,25},{9,1},{25,17},{2,10},{18... | collective-permute-start | bytes 786440 | tf_op jit(solution)/shard_map/ppermute | solution.py:212
  16.3 6.7 %collective-permute-start.16 = (bf16[512,256]{1,0:T(8,128)(2,1)S(1)}, bf16[512,256]{1,0:T(8,128)(2,1)S(1)}, u32[]{:S(2)}, u32[]{:S(2)}) collective-permute-start(bf16[512,256]{1,0:T(8,128)(2,1)S(1)} %collective-permute-done.refs_4_), channel_id=1, source_target_pairs={{8,16},{16,8},{9,17},{17,9},{10,18},{18,10},{11,19},{19,11},{12,20... | collective-permute-start | bytes 786440 | tf_op jit(solution)/shard_map/ppermute | solution.py:213
  17.0 7.7 %collective-permute-start.8 = (bf16[512,256]{1,0:T(8,128)(2,1)S(1)}, bf16[512,256]{1,0:T(8,128)(2,1)S(1)}, u32[]{:S(2)}, u32[]{:S(2)}) collective-permute-start(bf16[512,256]{1,0:T(8,128)(2,1)S(1)} %collective-permute-done.refs_4_), channel_id=1, source_target_pairs={{0,8},{16,24},{8,0},{24,16},{1,9},{17,25},{9,1},{25,17},{2,10},{18... | collective-permute-start | bytes 786440 | tf_op jit(solution)/shard_map/ppermute | solution.py:212
  19.1 6.9 %collective-permute-start.19 = (bf16[512,256]{1,0:T(8,128)(2,1)S(1)}, bf16[512,256]{1,0:T(8,128)(2,1)S(1)}, u32[]{:S(2)}, u32[]{:S(2)}) collective-permute-start(bf16[512,256]{1,0:T(8,128)(2,1)S(1)} %collective-permute-done.3.refs_7_), channel_id=1, source_target_pairs={{8,16},{16,8},{9,17},{17,9},{10,18},{18,10},{11,19},{19,11},{12,20... | collective-permute-start | bytes 786440 | tf_op jit(solution)/shard_map/ppermute | solution.py:213
  21.0 8.1 %collective-permute-start.4 = (bf16[512,256]{1,0:T(8,128)(2,1)S(1)}, bf16[512,256]{1,0:T(8,128)(2,1)}, u32[]{:S(2)}, u32[]{:S(2)}) collective-permute-start(bf16[512,256]{1,0:T(8,128)(2,1)S(1)} %collective-permute-done.2.refs_6_), channel_id=1, source_target_pairs={{0,2},{2,4},{4,6},{6,7},{7,5},{5,3},{3,1},{1,0},{8,10},{10,12},{12... | collective-permute-start | bytes 786440 | tf_op jit(solution)/shard_map/ppermute | solution.py:205
  21.5 8.9 %collective-permute-start.5 = (bf16[512,256]{1,0:T(8,128)(2,1)S(1)}, bf16[512,256]{1,0:T(8,128)(2,1)}, u32[]{:S(2)}, u32[]{:S(2)}) collective-permute-start(bf16[512,256]{1,0:T(8,128)(2,1)S(1)} %collective-permute-done.3.refs_7_), channel_id=1, source_target_pairs={{2,0},{4,2},{6,4},{7,6},{5,7},{3,5},{1,3},{0,1},{10,8},{12,10},{14... | collective-permute-start | bytes 786440 | tf_op jit(solution)/shard_map/ppermute | solution.py:209
  23.0 14.9 %collective-permute-start.11 = (bf16[512,256]{1,0:T(8,128)(2,1)S(1)}, bf16[512,256]{1,0:T(8,128)(2,1)}, u32[]{:S(2)}, u32[]{:S(2)}) collective-permute-start(bf16[512,256]{1,0:T(8,128)(2,1)S(1)} %collective-permute-done.3.refs_7_), channel_id=1, source_target_pairs={{0,8},{16,24},{8,0},{24,16},{1,9},{17,25},{9,1},{25,17},{2,10},{18... | collective-permute-start | bytes 786440 | tf_op jit(solution)/shard_map/ppermute | solution.py:212
  24.7 15.5 %collective-permute-start.18 = (bf16[512,256]{1,0:T(8,128)(2,1)S(1)}, bf16[512,256]{1,0:T(8,128)(2,1)}, u32[]{:S(2)}, u32[]{:S(2)}) collective-permute-start(bf16[512,256]{1,0:T(8,128)(2,1)S(1)} %collective-permute-done.2.refs_6_), channel_id=1, source_target_pairs={{8,16},{16,8},{9,17},{17,9},{10,18},{18,10},{11,19},{19,11},{12,20... | collective-permute-start | bytes 786440 | tf_op jit(solution)/shard_map/ppermute | solution.py:213
  26.0 14.8 %collective-permute-start.10 = (bf16[512,256]{1,0:T(8,128)(2,1)S(1)}, bf16[512,256]{1,0:T(8,128)(2,1)}, u32[]{:S(2)}, u32[]{:S(2)}) collective-permute-start(bf16[512,256]{1,0:T(8,128)(2,1)S(1)} %collective-permute-done.2.refs_6_), channel_id=1, source_target_pairs={{0,8},{16,24},{8,0},{24,16},{1,9},{17,25},{9,1},{25,17},{2,10},{18... | collective-permute-start | bytes 786440 | tf_op jit(solution)/shard_map/ppermute | solution.py:212
  29.1 14.0 %collective-permute-start.6 = (bf16[512,256]{1,0:T(8,128)(2,1)}, bf16[512,256]{1,0:T(8,128)(2,1)}, u32[]{:S(2)}, u32[]{:S(2)}) collective-permute-start(bf16[512,256]{1,0:T(8,128)(2,1)} %collective-permute-done.4.refs_8_), channel_id=1, source_target_pairs={{0,2},{2,4},{4,6},{6,7},{7,5},{5,3},{3,1},{1,0},{8,10},{10,12},{12... | collective-permute-start | bytes 786440 | tf_op jit(solution)/shard_map/ppermute | solution.py:205
  30.4 13.3 %collective-permute-start.21 = (bf16[512,256]{1,0:T(8,128)(2,1)}, bf16[512,256]{1,0:T(8,128)(2,1)}, u32[]{:S(2)}, u32[]{:S(2)}) collective-permute-start(bf16[512,256]{1,0:T(8,128)(2,1)} %collective-permute-done.5.refs_9_), channel_id=1, source_target_pairs={{8,16},{16,8},{9,17},{17,9},{10,18},{18,10},{11,19},{19,11},{12,20... | collective-permute-start | bytes 786440 | tf_op jit(solution)/shard_map/ppermute | solution.py:213
  32.6 14.0 %all-to-all-start = ((bf16[8,64,256]{2,1,0:T(8,128)(2,1)}), bf16[8,64,256]{2,1,0:T(8,128)(2,1)S(1)}, u32[]{:S(2)}, u32[]{:S(2)}) async-start(bf16[8,64,256]{2,1,0:T(8,128)(2,1)} %bitcast.4), calls=%async_computation | async-start | bytes 524288 | tf_op jit(solution)/shard_map/all_to_all | solution.py:199
  37.9 8.7 %collective-permute-start.13 = (bf16[512,256]{1,0:T(8,128)(2,1)}, bf16[512,256]{1,0:T(8,128)(2,1)S(1)}, u32[]{:S(2)}, u32[]{:S(2)}) collective-permute-start(bf16[512,256]{1,0:T(8,128)(2,1)} %collective-permute-done.5.refs_9_), channel_id=1, source_target_pairs={{0,8},{16,24},{8,0},{24,16},{1,9},{17,25},{9,1},{25,17},{2,10},{18... | collective-permute-start | bytes 786440 | tf_op jit(solution)/shard_map/ppermute | solution.py:212
  40.2 6.5 %collective-permute-start.20 = (bf16[512,256]{1,0:T(8,128)(2,1)}, bf16[512,256]{1,0:T(8,128)(2,1)S(1)}, u32[]{:S(2)}, u32[]{:S(2)}) collective-permute-start(bf16[512,256]{1,0:T(8,128)(2,1)} %collective-permute-done.4.refs_8_), channel_id=1, source_target_pairs={{8,16},{16,8},{9,17},{17,9},{10,18},{18,10},{11,19},{19,11},{12,20... | collective-permute-start | bytes 786440 | tf_op jit(solution)/shard_map/ppermute | solution.py:213
  40.9 5.8 %collective-permute-start.12 = (bf16[512,256]{1,0:T(8,128)(2,1)}, bf16[512,256]{1,0:T(8,128)(2,1)S(1)}, u32[]{:S(2)}, u32[]{:S(2)}) collective-permute-start(bf16[512,256]{1,0:T(8,128)(2,1)} %collective-permute-done.4.refs_8_), channel_id=1, source_target_pairs={{0,8},{16,24},{8,0},{24,16},{1,9},{17,25},{9,1},{25,17},{2,10},{18... | collective-permute-start | bytes 786440 | tf_op jit(solution)/shard_map/ppermute | solution.py:212
  58.7 24.4 %all-to-all-start.1 = ((bf16[8,144,256]{2,1,0:T(8,128)(2,1)}), bf16[8,144,256]{2,1,0:T(8,128)(2,1)S(1)}, u32[]{:S(2)}, u32[]{:S(2)}) async-start(bf16[8,144,256]{2,1,0:T(8,128)(2,1)} %get-tuple-element.9), calls=%async_computation.1 | async-start | bytes 1179648 | tf_op jit(solution)/shard_map/all_to_all | solution.py:242
  65.3 6.4 %collective-permute-start.24 = (f32[8,128]{1,0:T(8,128)S(1)}, f32[8,128]{1,0:T(8,128)S(1)}, u32[]{:S(2)}, u32[]{:S(2)}) collective-permute-start(f32[8,128]{1,0:T(8,128)S(1)} %copy-done.21), channel_id=1, source_target_pairs={{0,16},{8,24},{16,0},{24,8},{1,17},{9,25},{17,1},{25,9},{2,18},{10... | collective-permute-start | bytes 12296 | tf_op jit(solution)/shard_map/ppermute | solution.py:179
  (30 other events, 302.6 us)
where the time goes:
time: 86.3 us; the launch traced here: 85.8 us
  starting transfers between devices  57.2 us (66%)
  waiting for transfers between devices  11.2 us (13%)
  Pallas kernels  10.5 us (12%)
  local copies, waits for them, and re-layouts  4.51 us (5%)
  other arithmetic  1.46 us (2%)
  between operations  0.96 us (1%)
    ppermute x8, starting transfers between devices, per_device(): near = [lax.ppermute(c, 'rcv', swaps(0)) for c in chunks]  19.2 us
    ppermute x7, starting transfers between devices, summed(): lax.ppermute(x, axis, [(d, d ^ bit * m) for d in range(count)])  11.6 us
    pallas_call x1, Pallas kernels, per_device(): pl.pallas_call(functools.partial(maps_kernel, n_src, shifts), out_shape=(...  10.2 us
    ppermute x7, waiting for transfers between devices, summed(): lax.ppermute(x, axis, [(d, d ^ bit * m) for d in range(count)])  7.02 us
    ppermute x8, starting transfers between devices, per_device(): far = [lax.ppermute(c, 'rcv', swaps(1)) for c in chunks]  6.72 us
    ppermute x3, starting transfers between devices, per_device(): bwd = lax.ppermute(bwd, 'src', behind)  6.18 us
    all_to_all x1, starting transfers between devices, per_device(): images = lax.all_to_all(images, 'src', 0, 0, tiled=True)  5.72 us
    all_to_all x1, starting transfers between devices, per_device(): lax.all_to_all(start.reshape(n_src, blocks_here * rows, cols), 'src', 0,...  5.31 us
  transfers between devices with their start and end apart: 32, of which 9 were waited for; matrix products, arithmetic and copies ran while one was open for 2% of the time, Pallas kernels for 0%

commit v1 on v0

--- a/solution.py
+++ b/solution.py
@@ -37,17 +37,17 @@
 
 
 def maps_kernel(n_src, shifts, *refs):
-    me, band, field = refs[:3]
-    ends = [3, 3 + n_src, 3 + 2 * n_src, 3 + 3 * n_src]
+    band_in, field = refs[:2]
+    ends = [2, 2 + n_src, 2 + 2 * n_src, 2 + 3 * n_src]
     sources = [refs[a:b] for a, b in zip(ends[:-1], ends[1:])]
     grad, hess, images, sums_out = refs[ends[3] : ends[3] + 4]
-    held, lhs, every, factors, image0, image1, sems = refs[ends[3] + 4 :]
+    band, held, lhs, every, factors, image0, image1, sems, band_sem = refs[ends[3] + 4 :]
     blocks_here = grad.shape[0]
     rows = grad.shape[1] // 2
     cols = field.shape[2]
     half = cols // 2
     window = blocks_here * len(sources)
-    me_rcv, me_src = me[0], me[1]
+    me_rcv, me_src = lax.axis_index("rcv"), lax.axis_index("src")
     odd = lax.rem(me_rcv, 2)
     where = [ring_place(n_src, me_src, shift) for shift in shifts]
 
@@ -55,8 +55,11 @@
         [pltpu.make_async_copy(chunk, held.at[g, slot], sems.at[g, slot]) for slot, chunk in enumerate(group)]
         for g, group in enumerate(sources)
     ]
+    band_fetch = pltpu.make_async_copy(band_in, band, band_sem)
+    band_fetch.start()
     for fetch in sum(fetches, []):
         fetch.start()
+    band_fetch.wait()
 
     places = {}
     for i in range(blocks_here):
@@ -211,10 +214,8 @@
             shifts.append(step)
     near = [lax.ppermute(c, "rcv", swaps(0)) for c in chunks]
     far = [lax.ppermute(c, "rcv", swaps(1)) for c in chunks]
-    me = jnp.stack([lax.axis_index("rcv"), lax.axis_index("src")]).astype(jnp.int32)
-
     any_spec = pl.BlockSpec(memory_space=pl.ANY)
-    smem, vmem = pl.BlockSpec(memory_space=pltpu.SMEM), pl.BlockSpec(memory_space=pltpu.VMEM)
+    vmem = pl.BlockSpec(memory_space=pltpu.VMEM)
     band_cols = NEIGH * BLOCK
     grad, hess, images, sums = pl.pallas_call(
         functools.partial(maps_kernel, n_src, shifts),
@@ -224,9 +225,10 @@
             jax.ShapeDtypeStruct((n_src, 2 * blocks_here * rows + SHARE_ROWS, cols), jnp.bfloat16),
             jax.ShapeDtypeStruct((8, 128), jnp.float32),
         ),
-        in_specs=[smem, smem, vmem] + [any_spec] * (3 * n_src),
+        in_specs=[any_spec, vmem] + [any_spec] * (3 * n_src),
         out_specs=[vmem] * 4,
         scratch_shapes=[
+            pltpu.SMEM(band.shape, jnp.int32),
             pltpu.VMEM((3, n_src, blocks_here * BLOCK, cols), jnp.bfloat16),
             pltpu.VMEM((blocks_here * 2 * rows, n_src * cols), jnp.bfloat16),
             pltpu.VMEM((3 * blocks_here, blocks_here * 2 * rows, BLOCK), jnp.float32),
@@ -234,10 +236,11 @@
             pltpu.VMEM((n_src, blocks_here * rows, cols), jnp.float32),
             pltpu.VMEM((n_src, blocks_here * rows, cols), jnp.float32),
             pltpu.SemaphoreType.DMA((3, n_src)),
+            pltpu.SemaphoreType.DMA,
         ],
         compiler_params=pltpu.CompilerParams(vmem_limit_bytes=60 << 20),
         name="maps",
-    )(me, band, field, *chunks, *near, *far)
+    )(band, field, *chunks, *near, *far)
 
     images = lax.all_to_all(images, "src", 0, 0, tiled=True)
     sums = summed(summed(sums, "rcv", n_rcv), "src", n_src)

time: 86.3 us -> 86.4 us (level)
  transfers between devices with their start and end apart: 32 -> 32, of which waited for: 9 -> 9; matrix products, arithmetic and copies ran while one was open for 2% -> 1% of each run, Pallas kernels for 0% -> 0%
where the time goes in v1:
time: 86.4 us; the launch traced here: 85.8 us
  starting transfers between devices  57.3 us (66%)
  waiting for transfers between devices  11.7 us (14%)
  Pallas kernels  10.5 us (12%)
  local copies, waits for them, and re-layouts  4.48 us (5%)
  between operations  0.96 us (1%)
    ppermute x8, starting transfers between devices, per_device(): near = [lax.ppermute(c, 'rcv', swaps(0)) for c in chunks]  19.3 us
    ppermute x7, starting transfers between devices, summed(): lax.ppermute(x, axis, [(d, d ^ bit * m) for d in range(count)])  12 us
    pallas_call x1, Pallas kernels, per_device(): pl.pallas_call(functools.partial(maps_kernel, n_src, shifts), out_shape=(...  10.2 us
    ppermute x7, waiting for transfers between devices, summed(): lax.ppermute(x, axis, [(d, d ^ bit * m) for d in range(count)])  6.93 us
    ppermute x8, starting transfers between devices, per_device(): far = [lax.ppermute(c, 'rcv', swaps(1)) for c in chunks]  6.71 us
    ppermute x3, starting transfers between devices, per_device(): bwd = lax.ppermute(bwd, 'src', behind)  6.18 us
    all_to_all x1, starting transfers between devices, per_device(): images = lax.all_to_all(images, 'src', 0, 0, tiled=True)  5.48 us
    all_to_all x1, starting transfers between devices, per_device(): lax.all_to_all(start.reshape(n_src, blocks_here * rows, cols), 'src', 0,...  5.31 us
  transfers between devices with their start and end apart: 32, of which 9 were waited for; matrix products, arithmetic and copies ran while one was open for 1% of the time, Pallas kernels for 0%

profile of v1, /device:TPU:0, one launch (start us, length us, event | category | flops | bytes accessed | tf_op | source)
XLA Modules:
  0.0 85.8 jit_solution(12715298123017660626)
XLA Ops:
  1.7 3.0 %collective-permute-start.1 = (bf16[512,256]{1,0:T(8,128)(2,1)S(1)}, bf16[512,256]{1,0:T(8,128)(2,1)S(1)}, u32[]{:S(2)}, u32[]{:S(2)}) collective-permute-start(bf16[512,256]{1,0:T(8,128)(2,1)S(1)} %bitcast.26), channel_id=1, source_target_pairs={{2,0},{4,2},{6,4},{7,6},{5,7},{3,5},{1,3},{0,1},{10,8},{12,10},{14... | collective-permute-start | bytes 786440 | tf_op jit(solution)/shard_map/ppermute | solution.py:212
  5.5 3.3 %collective-permute-start.7 = (bf16[512,256]{1,0:T(8,128)(2,1)S(1)}, bf16[512,256]{1,0:T(8,128)(2,1)S(1)}, u32[]{:S(2)}, u32[]{:S(2)}) collective-permute-start(bf16[512,256]{1,0:T(8,128)(2,1)S(1)} %bitcast.29), channel_id=1, source_target_pairs={{0,8},{16,24},{8,0},{24,16},{1,9},{17,25},{9,1},{25,17},{2,10},{18... | collective-permute-start | bytes 786440 | tf_op jit(solution)/shard_map/ppermute | solution.py:215
  8.8 2.3 %collective-permute-done.1.refs_4_ = bf16[512,256]{1,0:T(8,128)(2,1)S(1)} collective-permute-done((bf16[512,256]{1,0:T(8,128)(2,1)S(1)}, bf16[512,256]{1,0:T(8,128)(2,1)S(1)}, u32[]{:S(2)}, u32[]{:S(2)}) %collective-permute-start.1) | collective-permute-done | bytes 262176 | tf_op jit(solution)/shard_map/ppermute | solution.py:212
  11.7 1.7 %collective-permute-start.3 = (bf16[512,256]{1,0:T(8,128)(2,1)S(1)}, bf16[512,256]{1,0:T(8,128)(2,1)S(1)}, u32[]{:S(2)}, u32[]{:S(2)}) collective-permute-start(bf16[512,256]{1,0:T(8,128)(2,1)S(1)} %collective-permute-done.1.refs_4_), channel_id=1, source_target_pairs={{2,0},{4,2},{6,4},{7,6},{5,7},{3,5},{1,3},{0,1},{10,8},{12,10},{14... | collective-permute-start | bytes 786440 | tf_op jit(solution)/shard_map/ppermute | solution.py:212
  13.8 2.5 %collective-permute-start.9 = (bf16[512,256]{1,0:T(8,128)(2,1)S(1)}, bf16[512,256]{1,0:T(8,128)(2,1)S(1)}, u32[]{:S(2)}, u32[]{:S(2)}) collective-permute-start(bf16[512,256]{1,0:T(8,128)(2,1)S(1)} %collective-permute-done.1.refs_4_), channel_id=1, source_target_pairs={{0,8},{16,24},{8,0},{24,16},{1,9},{17,25},{9,1},{25,17},{2,10},{18... | collective-permute-start | bytes 786440 | tf_op jit(solution)/shard_map/ppermute | solution.py:215
  17.0 2.1 %collective-permute-start.8 = (bf16[512,256]{1,0:T(8,128)(2,1)S(1)}, bf16[512,256]{1,0:T(8,128)(2,1)S(1)}, u32[]{:S(2)}, u32[]{:S(2)}) collective-permute-start(bf16[512,256]{1,0:T(8,128)(2,1)S(1)} %collective-permute-done.refs_3_), channel_id=1, source_target_pairs={{0,8},{16,24},{8,0},{24,16},{1,9},{17,25},{9,1},{25,17},{2,10},{18... | collective-permute-start | bytes 786440 | tf_op jit(solution)/shard_map/ppermute | solution.py:215
  21.5 1.5 %collective-permute-start.5 = (bf16[512,256]{1,0:T(8,128)(2,1)S(1)}, bf16[512,256]{1,0:T(8,128)(2,1)}, u32[]{:S(2)}, u32[]{:S(2)}) collective-permute-start(bf16[512,256]{1,0:T(8,128)(2,1)S(1)} %collective-permute-done.3.refs_6_), channel_id=1, source_target_pairs={{2,0},{4,2},{6,4},{7,6},{5,7},{3,5},{1,3},{0,1},{10,8},{12,10},{14... | collective-permute-start | bytes 786440 | tf_op jit(solution)/shard_map/ppermute | solution.py:212
  23.0 1.7 %collective-permute-start.11 = (bf16[512,256]{1,0:T(8,128)(2,1)S(1)}, bf16[512,256]{1,0:T(8,128)(2,1)}, u32[]{:S(2)}, u32[]{:S(2)}) collective-permute-start(bf16[512,256]{1,0:T(8,128)(2,1)S(1)} %collective-permute-done.3.refs_6_), channel_id=1, source_target_pairs={{0,8},{16,24},{8,0},{24,16},{1,9},{17,25},{9,1},{25,17},{2,10},{18... | collective-permute-start | bytes 786440 | tf_op jit(solution)/shard_map/ppermute | solution.py:215
  24.7 1.4 %collective-permute-start.18 = (bf16[512,256]{1,0:T(8,128)(2,1)S(1)}, bf16[512,256]{1,0:T(8,128)(2,1)}, u32[]{:S(2)}, u32[]{:S(2)}) collective-permute-start(bf16[512,256]{1,0:T(8,128)(2,1)S(1)} %collective-permute-done.2.refs_5_), channel_id=1, source_target_pairs={{8,16},{16,8},{9,17},{17,9},{10,18},{18,10},{11,19},{19,11},{12,20... | collective-permute-start | bytes 786440 | tf_op jit(solution)/shard_map/ppermute | solution.py:216
  26.0 3.0 %collective-permute-start.10 = (bf16[512,256]{1,0:T(8,128)(2,1)S(1)}, bf16[512,256]{1,0:T(8,128)(2,1)}, u32[]{:S(2)}, u32[]{:S(2)}) collective-permute-start(bf16[512,256]{1,0:T(8,128)(2,1)S(1)} %collective-permute-done.2.refs_5_), channel_id=1, source_target_pairs={{0,8},{16,24},{8,0},{24,16},{1,9},{17,25},{9,1},{25,17},{2,10},{18... | collective-permute-start | bytes 786440 | tf_op jit(solution)/shard_map/ppermute | solution.py:215
  29.1 1.3 %collective-permute-start.6 = (bf16[512,256]{1,0:T(8,128)(2,1)}, bf16[512,256]{1,0:T(8,128)(2,1)}, u32[]{:S(2)}, u32[]{:S(2)}) collective-permute-start(bf16[512,256]{1,0:T(8,128)(2,1)} %collective-permute-done.4.refs_7_), channel_id=1, source_target_pairs={{0,2},{2,4},{4,6},{6,7},{7,5},{5,3},{3,1},{1,0},{8,10},{10,12},{12... | collective-permute-start | bytes 786440 | tf_op jit(solution)/shard_map/ppermute | solution.py:208
  30.4 1.3 %collective-permute-start.21 = (bf16[512,256]{1,0:T(8,128)(2,1)}, bf16[512,256]{1,0:T(8,128)(2,1)}, u32[]{:S(2)}, u32[]{:S(2)}) collective-permute-start(bf16[512,256]{1,0:T(8,128)(2,1)} %collective-permute-done.5.refs_8_), channel_id=1, source_target_pairs={{8,16},{16,8},{9,17},{17,9},{10,18},{18,10},{11,19},{19,11},{12,20... | collective-permute-start | bytes 786440 | tf_op jit(solution)/shard_map/ppermute | solution.py:216
  32.6 5.3 %all-to-all-start = ((bf16[8,64,256]{2,1,0:T(8,128)(2,1)}), bf16[8,64,256]{2,1,0:T(8,128)(2,1)S(1)}, u32[]{:S(2)}, u32[]{:S(2)}) async-start(bf16[8,64,256]{2,1,0:T(8,128)(2,1)} %bitcast.2), calls=%async_computation | async-start | bytes 524288 | tf_op jit(solution)/shard_map/all_to_all | solution.py:202
  37.9 2.3 %collective-permute-start.13 = (bf16[512,256]{1,0:T(8,128)(2,1)}, bf16[512,256]{1,0:T(8,128)(2,1)S(1)}, u32[]{:S(2)}, u32[]{:S(2)}) collective-permute-start(bf16[512,256]{1,0:T(8,128)(2,1)} %collective-permute-done.5.refs_8_), channel_id=1, source_target_pairs={{0,8},{16,24},{8,0},{24,16},{1,9},{17,25},{9,1},{25,17},{2,10},{18... | collective-permute-start | bytes 786440 | tf_op jit(solution)/shard_map/ppermute | solution.py:215
  40.9 2.1 %collective-permute-start.12 = (bf16[512,256]{1,0:T(8,128)(2,1)}, bf16[512,256]{1,0:T(8,128)(2,1)S(1)}, u32[]{:S(2)}, u32[]{:S(2)}) collective-permute-start(bf16[512,256]{1,0:T(8,128)(2,1)} %collective-permute-done.4.refs_7_), channel_id=1, source_target_pairs={{0,8},{16,24},{8,0},{24,16},{1,9},{17,25},{9,1},{25,17},{2,10},{18... | collective-permute-start | bytes 786440 | tf_op jit(solution)/shard_map/ppermute | solution.py:215
  43.7 2.3 %collective-permute-start.14 = (bf16[512,256]{1,0:T(8,128)(2,1)}, bf16[512,256]{1,0:T(8,128)(2,1)S(1)}, u32[]{:S(2)}, u32[]{:S(2)}) collective-permute-start(bf16[512,256]{1,0:T(8,128)(2,1)} %collective-permute-done.6.refs_9_), channel_id=1, source_target_pairs={{0,8},{16,24},{8,0},{24,16},{1,9},{17,25},{9,1},{25,17},{2,10},{18... | collective-permute-start | bytes 786440 | tf_op jit(solution)/shard_map/ppermute | solution.py:215
  48.4 10.2 %maps.1 = (f32[2,64,768]{2,1,0:T(8,128)}, f32[2,64,768]{2,1,0:T(8,128)}, bf16[8,144,256]{2,1,0:T(8,128)(2,1)}, f32[8,128]{1,0:T(8,128)}) custom-call(s32[2,3]{1,0:T(2,128)} %refs_0_.1, bf16[8,64,256]{2,1,0:T(8,128)(2,1)} %copy-done.4, bf16[512,256]{1,0:T(8,128)(2,1)} %bitcast.30, bf16[512,256]{1,0:T(8,128)(2,1)} %copy-done.6, bf16[512,256]{1,0:T(8,128)(2,1)} %copy-done.5, ...), custom_call_target="tpu_custom_call" | custom-call | tf_op jit(solution)/shard_map/maps/pallas_call | solution.py:220
  58.6 5.5 %all-to-all-start.1 = ((bf16[8,144,256]{2,1,0:T(8,128)(2,1)}), bf16[8,144,256]{2,1,0:T(8,128)(2,1)S(1)}, u32[]{:S(2)}, u32[]{:S(2)}) async-start(bf16[8,144,256]{2,1,0:T(8,128)(2,1)} %get-tuple-element.9), calls=%async_computation.1 | async-start | bytes 1179648 | tf_op jit(solution)/shard_map/all_to_all | solution.py:245
  65.0 5.1 %collective-permute-start.24 = (f32[8,128]{1,0:T(8,128)S(1)}, f32[8,128]{1,0:T(8,128)S(1)}, u32[]{:S(2)}, u32[]{:S(2)}) collective-permute-start(f32[8,128]{1,0:T(8,128)S(1)} %copy-done.21), channel_id=1, source_target_pairs={{0,16},{8,24},{16,0},{24,8},{1,17},{9,25},{17,1},{25,9},{2,18},{10... | collective-permute-start | bytes 12296 | tf_op jit(solution)/shard_map/ppermute | solution.py:182
  70.1 1.6 %collective-permute-done.24 = f32[8,128]{1,0:T(8,128)S(1)} collective-permute-done((f32[8,128]{1,0:T(8,128)S(1)}, f32[8,128]{1,0:T(8,128)S(1)}, u32[]{:S(2)}, u32[]{:S(2)}) %collective-permute-start.24) | collective-permute-done | bytes 4128 | tf_op jit(solution)/shard_map/ppermute | solution.py:182
  71.7 2.6 %collective-permute-start.28 = (f32[8,128]{1,0:T(8,128)S(1)}, f32[8,128]{1,0:T(8,128)S(1)}, u32[]{:S(2)}, u32[]{:S(2)}) collective-permute-start(f32[8,128]{1,0:T(8,128)S(1)} %add_add_fusion.1), channel_id=1, source_target_pairs={{0,3},{1,2},{2,1},{3,0},{4,7},{5,6},{6,5},{7,4},{8,11},{9,10},{10,... | collective-permute-start | bytes 12296 | tf_op jit(solution)/shard_map/ppermute | solution.py:182
  76.3 1.7 %collective-permute-done.27 = f32[8,128]{1,0:T(8,128)S(1)} collective-permute-done((f32[8,128]{1,0:T(8,128)S(1)}, f32[8,128]{1,0:T(8,128)S(1)}, u32[]{:S(2)}, u32[]{:S(2)}) %collective-permute-start.27) | collective-permute-done | bytes 4128 | tf_op jit(solution)/shard_map/ppermute | solution.py:182
  78.5 2.4 %collective-permute-start.29 = (f32[8,128]{1,0:T(8,128)S(1)}, f32[8,128]{1,0:T(8,128)S(1)}, u32[]{:S(2)}, u32[]{:S(2)}) collective-permute-start(f32[8,128]{1,0:T(8,128)S(1)} %add_add_fusion), channel_id=1, source_target_pairs={{0,4},{1,5},{2,6},{3,7},{4,0},{5,1},{6,2},{7,3},{8,12},{9,13},{10,... | collective-permute-start | bytes 12296 | tf_op jit(solution)/shard_map/ppermute | solution.py:182
  81.0 2.1 %collective-permute-done.29 = f32[8,128]{1,0:T(8,128)S(1)} collective-permute-done((f32[8,128]{1,0:T(8,128)S(1)}, f32[8,128]{1,0:T(8,128)S(1)}, u32[]{:S(2)}, u32[]{:S(2)}) %collective-permute-start.29) | collective-permute-done | bytes 4128 | tf_op jit(solution)/shard_map/ppermute | solution.py:182
  (97 shorter events, 16.6 us)
Async XLA Ops:
  1.7 9.4 %collective-permute-start.1 = (bf16[512,256]{1,0:T(8,128)(2,1)S(1)}, bf16[512,256]{1,0:T(8,128)(2,1)S(1)}, u32[]{:S(2)}, u32[]{:S(2)}) collective-permute-start(bf16[512,256]{1,0:T(8,128)(2,1)S(1)} %bitcast.26), channel_id=1, source_target_pairs={{2,0},{4,2},{6,4},{7,6},{5,7},{3,5},{1,3},{0,1},{10,8},{12,10},{14... | collective-permute-start | bytes 786440 | tf_op jit(solution)/shard_map/ppermute | solution.py:212
  4.7 8.8 %collective-permute-start = (bf16[512,256]{1,0:T(8,128)(2,1)S(1)}, bf16[512,256]{1,0:T(8,128)(2,1)S(1)}, u32[]{:S(2)}, u32[]{:S(2)}) collective-permute-start(bf16[512,256]{1,0:T(8,128)(2,1)S(1)} %bitcast.27), channel_id=1, source_target_pairs={{0,2},{2,4},{4,6},{6,7},{7,5},{5,3},{3,1},{1,0},{8,10},{10,12},{12... | collective-permute-start | bytes 786440 | tf_op jit(solution)/shard_map/ppermute | solution.py:208
  4.8 9.0 %collective-permute-start.15 = (bf16[512,256]{1,0:T(8,128)(2,1)S(1)}, bf16[512,256]{1,0:T(8,128)(2,1)S(1)}, u32[]{:S(2)}, u32[]{:S(2)}) collective-permute-start(bf16[512,256]{1,0:T(8,128)(2,1)S(1)} %bitcast.28), channel_id=1, source_target_pairs={{8,16},{16,8},{9,17},{17,9},{10,18},{18,10},{11,19},{19,11},{12,20... | collective-permute-start | bytes 786440 | tf_op jit(solution)/shard_map/ppermute | solution.py:216
  5.5 10.8 %collective-permute-start.7 = (bf16[512,256]{1,0:T(8,128)(2,1)S(1)}, bf16[512,256]{1,0:T(8,128)(2,1)S(1)}, u32[]{:S(2)}, u32[]{:S(2)}) collective-permute-start(bf16[512,256]{1,0:T(8,128)(2,1)S(1)} %bitcast.29), channel_id=1, source_target_pairs={{0,8},{16,24},{8,0},{24,16},{1,9},{17,25},{9,1},{25,17},{2,10},{18... | collective-permute-start | bytes 786440 | tf_op jit(solution)/shard_map/ppermute | solution.py:215
  11.1 5.9 %collective-permute-start.17 = (bf16[512,256]{1,0:T(8,128)(2,1)S(1)}, bf16[512,256]{1,0:T(8,128)(2,1)S(1)}, u32[]{:S(2)}, u32[]{:S(2)}) collective-permute-start(bf16[512,256]{1,0:T(8,128)(2,1)S(1)} %collective-permute-done.1.refs_4_), channel_id=1, source_target_pairs={{8,16},{16,8},{9,17},{17,9},{10,18},{18,10},{11,19},{19,11},{12,20... | collective-permute-start | bytes 786440 | tf_op jit(solution)/shard_map/ppermute | solution.py:216
  11.7 7.4 %collective-permute-start.3 = (bf16[512,256]{1,0:T(8,128)(2,1)S(1)}, bf16[512,256]{1,0:T(8,128)(2,1)S(1)}, u32[]{:S(2)}, u32[]{:S(2)}) collective-permute-start(bf16[512,256]{1,0:T(8,128)(2,1)S(1)} %collective-permute-done.1.refs_4_), channel_id=1, source_target_pairs={{2,0},{4,2},{6,4},{7,6},{5,7},{3,5},{1,3},{0,1},{10,8},{12,10},{14... | collective-permute-start | bytes 786440 | tf_op jit(solution)/shard_map/ppermute | solution.py:212
  13.5 7.5 %collective-permute-start.2 = (bf16[512,256]{1,0:T(8,128)(2,1)S(1)}, bf16[512,256]{1,0:T(8,128)(2,1)S(1)}, u32[]{:S(2)}, u32[]{:S(2)}) collective-permute-start(bf16[512,256]{1,0:T(8,128)(2,1)S(1)} %collective-permute-done.refs_3_), channel_id=1, source_target_pairs={{0,2},{2,4},{4,6},{6,7},{7,5},{5,3},{3,1},{1,0},{8,10},{10,12},{12... | collective-permute-start | bytes 786440 | tf_op jit(solution)/shard_map/ppermute | solution.py:208
  13.8 7.7 %collective-permute-start.9 = (bf16[512,256]{1,0:T(8,128)(2,1)S(1)}, bf16[512,256]{1,0:T(8,128)(2,1)S(1)}, u32[]{:S(2)}, u32[]{:S(2)}) collective-permute-start(bf16[512,256]{1,0:T(8,128)(2,1)S(1)} %collective-permute-done.1.refs_4_), channel_id=1, source_target_pairs={{0,8},{16,24},{8,0},{24,16},{1,9},{17,25},{9,1},{25,17},{2,10},{18... | collective-permute-start | bytes 786440 | tf_op jit(solution)/shard_map/ppermute | solution.py:215
  16.3 6.7 %collective-permute-start.16 = (bf16[512,256]{1,0:T(8,128)(2,1)S(1)}, bf16[512,256]{1,0:T(8,128)(2,1)S(1)}, u32[]{:S(2)}, u32[]{:S(2)}) collective-permute-start(bf16[512,256]{1,0:T(8,128)(2,1)S(1)} %collective-permute-done.refs_3_), channel_id=1, source_target_pairs={{8,16},{16,8},{9,17},{17,9},{10,18},{18,10},{11,19},{19,11},{12,20... | collective-permute-start | bytes 786440 | tf_op jit(solution)/shard_map/ppermute | solution.py:216
  17.0 7.7 %collective-permute-start.8 = (bf16[512,256]{1,0:T(8,128)(2,1)S(1)}, bf16[512,256]{1,0:T(8,128)(2,1)S(1)}, u32[]{:S(2)}, u32[]{:S(2)}) collective-permute-start(bf16[512,256]{1,0:T(8,128)(2,1)S(1)} %collective-permute-done.refs_3_), channel_id=1, source_target_pairs={{0,8},{16,24},{8,0},{24,16},{1,9},{17,25},{9,1},{25,17},{2,10},{18... | collective-permute-start | bytes 786440 | tf_op jit(solution)/shard_map/ppermute | solution.py:215
  19.1 6.9 %collective-permute-start.19 = (bf16[512,256]{1,0:T(8,128)(2,1)S(1)}, bf16[512,256]{1,0:T(8,128)(2,1)S(1)}, u32[]{:S(2)}, u32[]{:S(2)}) collective-permute-start(bf16[512,256]{1,0:T(8,128)(2,1)S(1)} %collective-permute-done.3.refs_6_), channel_id=1, source_target_pairs={{8,16},{16,8},{9,17},{17,9},{10,18},{18,10},{11,19},{19,11},{12,20... | collective-permute-start | bytes 786440 | tf_op jit(solution)/shard_map/ppermute | solution.py:216
  21.0 8.1 %collective-permute-start.4 = (bf16[512,256]{1,0:T(8,128)(2,1)S(1)}, bf16[512,256]{1,0:T(8,128)(2,1)}, u32[]{:S(2)}, u32[]{:S(2)}) collective-permute-start(bf16[512,256]{1,0:T(8,128)(2,1)S(1)} %collective-permute-done.2.refs_5_), channel_id=1, source_target_pairs={{0,2},{2,4},{4,6},{6,7},{7,5},{5,3},{3,1},{1,0},{8,10},{10,12},{12... | collective-permute-start | bytes 786440 | tf_op jit(solution)/shard_map/ppermute | solution.py:208
  21.5 8.9 %collective-permute-start.5 = (bf16[512,256]{1,0:T(8,128)(2,1)S(1)}, bf16[512,256]{1,0:T(8,128)(2,1)}, u32[]{:S(2)}, u32[]{:S(2)}) collective-permute-start(bf16[512,256]{1,0:T(8,128)(2,1)S(1)} %collective-permute-done.3.refs_6_), channel_id=1, source_target_pairs={{2,0},{4,2},{6,4},{7,6},{5,7},{3,5},{1,3},{0,1},{10,8},{12,10},{14... | collective-permute-start | bytes 786440 | tf_op jit(solution)/shard_map/ppermute | solution.py:212
  23.0 14.9 %collective-permute-start.11 = (bf16[512,256]{1,0:T(8,128)(2,1)S(1)}, bf16[512,256]{1,0:T(8,128)(2,1)}, u32[]{:S(2)}, u32[]{:S(2)}) collective-permute-start(bf16[512,256]{1,0:T(8,128)(2,1)S(1)} %collective-permute-done.3.refs_6_), channel_id=1, source_target_pairs={{0,8},{16,24},{8,0},{24,16},{1,9},{17,25},{9,1},{25,17},{2,10},{18... | collective-permute-start | bytes 786440 | tf_op jit(solution)/shard_map/ppermute | solution.py:215
  24.7 15.5 %collective-permute-start.18 = (bf16[512,256]{1,0:T(8,128)(2,1)S(1)}, bf16[512,256]{1,0:T(8,128)(2,1)}, u32[]{:S(2)}, u32[]{:S(2)}) collective-permute-start(bf16[512,256]{1,0:T(8,128)(2,1)S(1)} %collective-permute-done.2.refs_5_), channel_id=1, source_target_pairs={{8,16},{16,8},{9,17},{17,9},{10,18},{18,10},{11,19},{19,11},{12,20... | collective-permute-start | bytes 786440 | tf_op jit(solution)/shard_map/ppermute | solution.py:216
  26.0 14.8 %collective-permute-start.10 = (bf16[512,256]{1,0:T(8,128)(2,1)S(1)}, bf16[512,256]{1,0:T(8,128)(2,1)}, u32[]{:S(2)}, u32[]{:S(2)}) collective-permute-start(bf16[512,256]{1,0:T(8,128)(2,1)S(1)} %collective-permute-done.2.refs_5_), channel_id=1, source_target_pairs={{0,8},{16,24},{8,0},{24,16},{1,9},{17,25},{9,1},{25,17},{2,10},{18... | collective-permute-start | bytes 786440 | tf_op jit(solution)/shard_map/ppermute | solution.py:215
  29.1 14.0 %collective-permute-start.6 = (bf16[512,256]{1,0:T(8,128)(2,1)}, bf16[512,256]{1,0:T(8,128)(2,1)}, u32[]{:S(2)}, u32[]{:S(2)}) collective-permute-start(bf16[512,256]{1,0:T(8,128)(2,1)} %collective-permute-done.4.refs_7_), channel_id=1, source_target_pairs={{0,2},{2,4},{4,6},{6,7},{7,5},{5,3},{3,1},{1,0},{8,10},{10,12},{12... | collective-permute-start | bytes 786440 | tf_op jit(solution)/shard_map/ppermute | solution.py:208
  30.4 13.3 %collective-permute-start.21 = (bf16[512,256]{1,0:T(8,128)(2,1)}, bf16[512,256]{1,0:T(8,128)(2,1)}, u32[]{:S(2)}, u32[]{:S(2)}) collective-permute-start(bf16[512,256]{1,0:T(8,128)(2,1)} %collective-permute-done.5.refs_8_), channel_id=1, source_target_pairs={{8,16},{16,8},{9,17},{17,9},{10,18},{18,10},{11,19},{19,11},{12,20... | collective-permute-start | bytes 786440 | tf_op jit(solution)/shard_map/ppermute | solution.py:216
  32.6 14.0 %all-to-all-start = ((bf16[8,64,256]{2,1,0:T(8,128)(2,1)}), bf16[8,64,256]{2,1,0:T(8,128)(2,1)S(1)}, u32[]{:S(2)}, u32[]{:S(2)}) async-start(bf16[8,64,256]{2,1,0:T(8,128)(2,1)} %bitcast.2), calls=%async_computation | async-start | bytes 524288 | tf_op jit(solution)/shard_map/all_to_all | solution.py:202
  37.9 8.7 %collective-permute-start.13 = (bf16[512,256]{1,0:T(8,128)(2,1)}, bf16[512,256]{1,0:T(8,128)(2,1)S(1)}, u32[]{:S(2)}, u32[]{:S(2)}) collective-permute-start(bf16[512,256]{1,0:T(8,128)(2,1)} %collective-permute-done.5.refs_8_), channel_id=1, source_target_pairs={{0,8},{16,24},{8,0},{24,16},{1,9},{17,25},{9,1},{25,17},{2,10},{18... | collective-permute-start | bytes 786440 | tf_op jit(solution)/shard_map/ppermute | solution.py:215
  40.2 6.4 %collective-permute-start.20 = (bf16[512,256]{1,0:T(8,128)(2,1)}, bf16[512,256]{1,0:T(8,128)(2,1)S(1)}, u32[]{:S(2)}, u32[]{:S(2)}) collective-permute-start(bf16[512,256]{1,0:T(8,128)(2,1)} %collective-permute-done.4.refs_7_), channel_id=1, source_target_pairs={{8,16},{16,8},{9,17},{17,9},{10,18},{18,10},{11,19},{19,11},{12,20... | collective-permute-start | bytes 786440 | tf_op jit(solution)/shard_map/ppermute | solution.py:216
  58.6 24.4 %all-to-all-start.1 = ((bf16[8,144,256]{2,1,0:T(8,128)(2,1)}), bf16[8,144,256]{2,1,0:T(8,128)(2,1)S(1)}, u32[]{:S(2)}, u32[]{:S(2)}) async-start(bf16[8,144,256]{2,1,0:T(8,128)(2,1)} %get-tuple-element.9), calls=%async_computation.1 | async-start | bytes 1179648 | tf_op jit(solution)/shard_map/all_to_all | solution.py:245
  64.1 6.0 %collective-permute-start.25 = (f32[8,128]{1,0:T(8,128)S(1)}, f32[8,128]{1,0:T(8,128)S(1)}, u32[]{:S(2)}, u32[]{:S(2)}) collective-permute-start(f32[8,128]{1,0:T(8,128)S(1)} %copy-done.21), channel_id=1, source_target_pairs={{0,24},{8,16},{16,8},{24,0},{1,25},{9,17},{17,9},{25,1},{2,26},{10... | collective-permute-start | bytes 12296 | tf_op jit(solution)/shard_map/ppermute | solution.py:182
  65.0 6.7 %collective-permute-start.24 = (f32[8,128]{1,0:T(8,128)S(1)}, f32[8,128]{1,0:T(8,128)S(1)}, u32[]{:S(2)}, u32[]{:S(2)}) collective-permute-start(f32[8,128]{1,0:T(8,128)S(1)} %copy-done.21), channel_id=1, source_target_pairs={{0,16},{8,24},{16,0},{24,8},{1,17},{9,25},{17,1},{25,9},{2,18},{10... | collective-permute-start | bytes 12296 | tf_op jit(solution)/shard_map/ppermute | solution.py:182
  (30 other events, 302.3 us)
